TPU v7x, 32 devices: a whole 2x2x4 slice. The times are simulated.
32 devices in a mesh: row: 4 (over y, x), col: 8 (over z, core).
Axes of the slice: x: 2, y: 2, z: 4, core: 2. Of those that a mesh axis runs over, the one named last changes fastest.
Arguments:
- grad_out: bfloat16 [4096, 512], P(('row', 'col'))
- relu_mask: int32 [4096, 512], P(('row', 'col')), may hold values 0 or 1
- aggregated: bfloat16 [4096, 512], P(('row', 'col')), may hold values from -6 to 6
- weight: bfloat16 [512, 512], replicated, may hold values from -0.25 to 0.25
- adj_blocks: bfloat16 [4, 8, 5, 128, 128], P('row', 'col'), may hold values from 0 to 0.11867817
- block_pos: int32 [4, 8, 5], P('row', 'col'), may hold values from 0 to 31, as said below
- block_live: int32 [4, 8], P('row', 'col'), may hold values from 1 to 5, as said below
Outputs:
- grad_input: bfloat16 [8, 512, 512], P('col', 'row')
- grad_weight: float32 [512, 512], replicated
- grad_bias: float32 [512], replicated
Inputs may be any that keep to these rules, and one draw needn't show every extreme that they name: `block_pos`: within one tile the 5 slots name different positions; position p is block row p // 4, block column p % 4. `block_live`: some tile uses all 5 slots.
All inputs are finite; a program needn't handle non-finite values. No bound on the sum of `relu_mask` on one device may be relied on, other than what follows from the above.
Results may differ from a plain program's by a relative error of at most 0.005.
Values may be sent and summed in bfloat16 or wider, within the bound.
A program may use at most 64 MiB of HBM per device.

v0:
```python
import math

import jax
import jax.numpy as jnp
from jax import lax
from jax.sharding import PartitionSpec as P


def body(grad_out, relu_mask, aggregated, weight, adj_blocks, block_pos, block_live):
    rows_dev, feat_dim = grad_out.shape
    grad_pre = grad_out * relu_mask.astype(jnp.bfloat16)
    projected = jnp.einsum(
        "ng,fg->nf", grad_pre, weight, preferred_element_type=jnp.float32
    ).astype(jnp.bfloat16)
    row_block = lax.all_gather(projected, "col", axis=0, tiled=True)
    blocks = adj_blocks[0, 0]
    positions = block_pos[0, 0]
    live_count = block_live[0, 0]
    capacity = blocks.shape[0]
    block_width = blocks.shape[-1]
    tile_cols = lax.axis_size("row") * rows_dev // block_width
    tile_row_count = row_block.shape[0] // block_width
    stacked_tiles = row_block.reshape(tile_row_count, block_width, feat_dim)
    group_size = max((divisor for divisor in range(1, 17) if capacity % divisor == 0))
    group_turns = capacity // group_size
    column_ids = jnp.arange(tile_cols, dtype=jnp.int32)

    def add_group(running_total, turn_index):
        first_slot = turn_index * group_size
        part_blocks = lax.dynamic_slice_in_dim(blocks, first_slot, group_size, 0)
        part_slots = lax.dynamic_slice_in_dim(positions, first_slot, group_size, 0)
        selected_row_set = stacked_tiles[part_slots // tile_cols]
        partial_products = jnp.einsum(
            "kab,kaf->kbf", part_blocks, selected_row_set, preferred_element_type=jnp.float32
        )
        alive = first_slot + jnp.arange(group_size, dtype=jnp.int32) < live_count
        insert_position = ((part_slots % tile_cols)[:, None] == column_ids[None, :]) & alive[
            :, None
        ]
        update = jnp.einsum(
            "lj,lsu->jsu",
            insert_position.astype(jnp.float32),
            partial_products,
            precision=lax.Precision.HIGHEST,
        )
        return (running_total + update, None)

    start_sum = jnp.zeros((tile_cols, block_width, feat_dim), jnp.float32)
    running_total, _ = lax.scan(add_group, start_sum, jnp.arange(group_turns, dtype=jnp.int32))
    column_terms = running_total.reshape(tile_cols * block_width, feat_dim)
    summed = lax.psum_scatter(column_terms, "row", scatter_dimension=0, tiled=True)
    grad_input = summed.astype(jnp.bfloat16).reshape(1, rows_dev, feat_dim)
    weight_terms = jnp.einsum("nf,ng->fg", aggregated, grad_pre, preferred_element_type=jnp.float32)
    bias_terms = jnp.sum(grad_pre.astype(jnp.float32), axis=0)
    factor = 1.0 / math.sqrt(rows_dev * lax.axis_size("row") * lax.axis_size("col"))
    weight_gradient_total, bias_total = lax.psum((weight_terms, bias_terms), ("row", "col"))
    return (grad_input, weight_gradient_total * factor, bias_total * factor)


def solution(mesh):
    return jax.shard_map(
        body,
        mesh=mesh,
        in_specs=(
            P(("row", "col"), None),
            P(("row", "col"), None),
            P(("row", "col"), None),
            P(),
            P("row", "col", None, None, None),
            P("row", "col", None),
            P("row", "col"),
        ),
        out_specs=(P("col", "row", None), P(), P()),
        check_vma=False,
    )
```

profile of v0, /device:TPU:0, one launch (start us, length us, event | category | flops | bytes accessed | tf_op | source)
XLA Modules:
  0.0 162.6 jit_solution(17887377880358279071)
XLA Ops:
  8.0 0.0 copy-start
  8.0 0.0 copy-start.2
  8.0 0.0 all-gather.2.cloned.1.call-start
  8.1 1.1 convert_reduce_fusion
  9.2 0.0 copy-done
  9.2 1.0 convolution_convert_fusion
  10.2 0.0 copy-start.1
  10.2 0.0 all-gather.2.cloned.1.call-update
  10.2 0.0 all-reduce.2.cloned.1.call-start
  10.2 2.2 %convolution_bitcast_fusion = f32[512,512]{0,1:T(8,128)} fusion(bf16[128,512]{1,0:T(8,128)(2,1)S(1)} %get-tuple-element.31, bf16[128,512]{1,0:T(8,128)(2,1)} %param.9), kind=kOutput, calls=%fused_computation.3 | convolution fusion | flops 67108864 | bytes 1310720 | tf_op jit(solution)/shard_map/nf,ng->fg/dot_general | solution.py:53
  12.4 0.0 all-reduce.2.cloned.1.call-update
  12.5 0.0 reduce-scatter.2.cloned.1.call-start
  12.5 0.0 copy-done.2
  13.2 23.4 %all-gather.2.cloned.1.call-done = bf16[1024,512]{1,0:T(8,128)(2,1)} async-done(((bf16[128,512]{1,0:T(8,128)(2,1)}), bf16[1024,512]{1,0:T(8,128)(2,1)}) %all-gather.2.cloned.1.call-update) | async-done | bytes 1048592 | tf_op jit(solution)/shard_map/all_gather | solution.py:15
  36.6 1.8 %gather_fusion = bf16[5,128,512]{2,1,0:T(8,128)(2,1)S(1)} fusion(bf16[8,128,512]{2,1,0:T(8,128)(2,1)} %bitcast.37, s32[1024]{0:T(1024)S(1)} %pad_clamp_fusion), kind=kCustom, calls=%fused_computation | custom fusion | bytes 1310740 | tf_op jit(solution)/shard_map/while/body/eval_jaxpr/gather | solution.py:32
  38.5 0.0 copy-done.1
  38.5 1.4 fusion.2
  39.9 2.1 %copy.13 = f32[5,512,128]{1,0,2:T(8,128)S(1)} copy(f32[5,512,128]{2,1,0:T(8,128)} %fusion.2) | data formatting | bytes 2621440 | tf_op jit(solution)/shard_map/while/body/eval_jaxpr/kab,kaf->kbf/dot_general | solution.py:33
  42.1 1.1 fusion
  43.1 1.3 copy.11
  44.4 0.0 reduce-scatter.2.cloned.1.call-update
  44.5 39.9 %psum.15 = f32[512]{0:T(512)S(1)} all-reduce(f32[512]{0:T(512)S(1)} %get-tuple-element.30), channel_id=1, replica_groups=mesh['row'=4,'col'=8] {'row','col'}, use_global_device_ids=true, to_apply=%region_3.4 | all-reduce | flops 512 | bytes 4096 | tf_op jit(solution)/shard_map/psum | solution.py:56
  84.4 0.6 broadcast_multiply_fusion.1
  85.0 65.9 %all-reduce.2.cloned.1.call-done = f32[512,512]{0,1:T(8,128)} async-done(((f32[512,512]{0,1:T(8,128)}), f32[512,512]{0,1:T(8,128)}) %all-reduce.2.cloned.1.call-update) | async-done | bytes 1048592 | tf_op jit(solution)/shard_map/psum | solution.py:56
  150.9 1.3 broadcast_multiply_fusion
  152.2 1.3 copy.12
  153.5 0.0 reduce-scatter.2.cloned.1.call-done
  153.5 1.6 convert_bitcast_fusion
  (4 shorter events, 0.0 us)
Async XLA Ops:
  8.0 1.2 copy-start
  8.0 4.5 %copy-start.2 = (s32[1,1,5]{2,1,0:T(1,128)S(1)}, s32[1,1,5]{2,1,0:T(1,128)}, u32[]{:S(2)}) copy-start(s32[1,1,5]{2,1,0:T(1,128)} %param.12) | copy-start | bytes 64
  8.0 28.6 %all-gather.2.cloned.1.call-start = ((), (), s32[]{:S(2)}) async-start(), calls=%async_computation.1 | async-start | bytes 1179648 | tf_op jit(solution)/shard_map/all_gather | solution.py:15
  10.2 28.3 %copy-start.1 = (bf16[1,1,5,128,128]{4,3,2,1,0:T(8,128)(2,1)S(1)}, bf16[1,1,5,128,128]{4,3,2,1,0:T(8,128)(2,1)}, u32[]{:S(2)}) copy-start(bf16[1,1,5,128,128]{4,3,2,1,0:T(8,128)(2,1)} %param.11) | copy-start | bytes 491524
  10.2 140.7 %all-reduce.2.cloned.1.call-start = ((), (), s32[]{:S(2)}) async-start(), calls=%async_computation.3 | async-start | bytes 2097152 | tf_op jit(solution)/shard_map/psum | solution.py:56
  12.5 141.0 %reduce-scatter.2.cloned.1.call-start = ((), (), s32[]{:S(2)}) async-start(), calls=%async_computation.2 | async-start | bytes 1310720 | tf_op jit(solution)/shard_map/reduce_scatter | solution.py:51
Sparse Core Ops, SparseCore 0:
  11.0 25.5 all-gather.1
  44.6 27.9 reduce-scatter.1
Sparse Core Ops, SparseCore 1:
  17.3 133.5 all-reduce.1
where the time goes:
time: 163 us
  waiting for transfers between devices  89.3 us (55%)
  blocking collectives  39.9 us (24%)
  between operations  16.2 us (10%)
  local copies, waits for them, and re-layouts  6.57 us (4%)
  matrix products  5.7 us (3%)
  other arithmetic  4.67 us (3%)
    psum x1, waiting for transfers between devices, body(): lax.psum((weight_terms, bias_terms), ('row', 'col'))  65.9 us
    psum x1, blocking collectives, body(): lax.psum((weight_terms, bias_terms), ('row', 'col'))  39.9 us
    all_gather x1, waiting for transfers between devices, body(): row_block = lax.all_gather(projected, 'col', axis=0, tiled=True)  23.4 us
  transfers between devices with their start and end apart: 3, of which 2 were waited for; matrix products, arithmetic and copies ran while one was open for 8% of the time, Pallas kernels for 0%

commit v1 on v0

v1 whole, which is shorter than its diff:
```python
import functools
import math

import jax
import jax.numpy as jnp
from jax import lax
from jax.experimental import pallas as pl
from jax.experimental.pallas import tpu as pltpu
from jax.sharding import PartitionSpec as P

MESH = pl.DeviceIdType.MESH
BF = jnp.bfloat16
F32 = jnp.float32
TILE = 16


def dot0(a, b):
    return lax.dot_general(a, b, (((0,), (0,)), ((), ())), preferred_element_type=F32)


def kernel(cfg, go_ref, mask_ref, agg_ref, w_ref, blk_ref, pos_ref, live_ref,
           gi_ref, gw_ref, gb_ref, *scr):
    n_row, n_col, nch, cap, group, scatter = cfg
    n_z = n_col // 2
    gath = scr[:nch]
    lhs, cbuf, rbuf, asib, gpart, grecv, zsend, zrecv, gw = scr[nch:nch + 9]
    ag_s, ag_r, fw_s, fw_r, c_s, c_r, as_s, as_r, g_s, g_r, z_s, z_r, wz_s, wz_r, wr_s, wr_r, wf_s, wf_r = scr[nch + 9:]
    rows, feat = go_ref.shape
    fc = feat // nch
    blk = blk_ref.shape[-1]
    tbc = n_row * rows // blk
    half = feat // 2
    piece = half // n_row
    part = piece // n_z if scatter else piece
    me_r, me_c = lax.axis_index("row"), lax.axis_index("col")
    z, core = me_c // 2, me_c % 2
    sib = z * 2 + 1 - core
    sib_id = (me_r, sib)

    def row_id(d):
        return ((me_r + d) % n_row, me_c)

    def z_id(d):
        return (me_r, ((z + d) % n_z) * 2 + core)

    sent = []

    def send(src, dst, s, r, dev):
        c = pltpu.make_async_remote_copy(src_ref=src, dst_ref=dst, send_sem=s, recv_sem=r,
                                         device_id=dev, device_id_type=MESH)
        c.start()
        sent.append(c)
        return c

    barrier = pltpu.get_barrier_semaphore()
    peers = [sib_id] + [z_id(d) for d in range(1, n_z)] + [row_id(d) for d in range(1, n_row)]
    for p in peers:
        pl.semaphore_signal(barrier, inc=1, device_id=p, device_id_type=MESH)

    for ch in range(nch):
        cols = slice(ch * fc, (ch + 1) * fc)
        gath[ch][me_c] = go_ref[:, cols] * mask_ref[:, cols].astype(F32).astype(BF)

    pl.semaphore_wait(barrier, len(peers))

    sib_cp, z_cp = [], []
    other = pl.ds(pl.multiple_of((1 - core) * half, half), half)
    mine = pl.ds(pl.multiple_of(core * half, half), half)
    agg_cp = send(agg_ref.at[:, other], asib, as_s, as_r, sib_id)
    for ch in range(nch):
        own = gath[ch].at[me_c]
        sib_cp.append(send(own, own, ag_s.at[ch, 0], ag_r.at[ch, 0], sib_id))
        z_cp.append([send(own, own, ag_s.at[ch, d], ag_r.at[ch, d], z_id(d)) for d in range(1, n_z)])

    agg_cp.wait_recv()
    bias = jnp.zeros((1, feat), F32)
    sums = []
    for ch in range(nch):
        cols = slice(ch * fc, (ch + 1) * fc)
        sib_cp[ch].wait_recv()
        a, b = gath[ch][me_c], gath[ch][sib]
        g = dot0(agg_ref[:, mine], a) + dot0(asib[...], b)
        gpart[:, 0:piece, cols] = g.astype(BF).reshape(n_row, piece, fc)
        sums.append(jnp.sum(a.astype(F32) + b.astype(F32), axis=0, keepdims=True))
    bias = jnp.concatenate(sums, axis=1)

    def two_rows(v):
        hi = v.astype(BF).astype(F32)
        ids = lax.broadcasted_iota(jnp.int32, (TILE, feat), 0)
        return jnp.where(ids == 0, hi, jnp.where(ids == 1, v - hi, 0.0)).astype(BF)

    tail = two_rows(bias)
    for r in range(n_row):
        gpart[r, piece:piece + TILE, :] = tail
    g_cp = [send(gpart.at[(me_r + d) % n_row], grecv.at[d - 1], g_s.at[d - 1], g_r.at[d - 1], row_id(d))
            for d in range(1, n_row)]

    if cap == group:
        for k in range(cap):
            at = pos_ref[0, 0, k] % tbc
            alive = k < live_ref[0, 0]
            for j in range(tbc):
                lhs[k * blk:(k + 1) * blk, j * blk:(j + 1) * blk] = jnp.where(
                    alive & (at == j), blk_ref[0, 0, k], jnp.zeros((blk, blk), BF))

    for c in g_cp:
        c.wait_recv()
    acc = gpart[me_r].astype(F32)
    for d in range(1, n_row):
        acc += grecv[d - 1].astype(F32)
    tail = two_rows(jnp.sum(acc[piece:], axis=0, keepdims=True))
    if scatter:
        zsend[:, 0:part] = acc[:piece].astype(BF).reshape(n_z, part, feat)
        for q in range(n_z):
            zsend[q, part:] = tail
    else:
        zsend[0, 0:part] = acc[:piece].astype(BF)
        zsend[0, part:] = tail
    zpick = [zsend.at[(z + d) % n_z if scatter else 0] for d in range(n_z)]
    zz_cp = [send(zpick[d], zrecv.at[d - 1], z_s.at[d - 1], z_r.at[d - 1], z_id(d)) for d in range(1, n_z)]

    def forward(ch):
        out = []
        for d in range(1, n_z):
            z_cp[ch][d - 1].wait_recv()
            slot = gath[ch].at[((z + n_z - d) % n_z) * 2 + core]
            out.append(send(slot, slot, fw_s.at[ch, d - 1], fw_r.at[ch, d - 1], sib_id))
        return out

    def contribute(ch, fw):
        for c in fw:
            c.wait_recv()
        if cap == group:
            rhs = jnp.concatenate([gath[ch][pos_ref[0, 0, k] // tbc] for k in range(cap)], axis=0)
            cbuf[ch] = dot0(lhs[...], rhs).astype(BF).reshape(n_row, rows, fc)
        else:
            acc_ref = lhs
            acc_ref[...] = jnp.zeros_like(acc_ref)

            def turn(t, carry):
                for i in range(group):
                    k = t * group + i
                    p = pos_ref[0, 0, k]
                    rhs = gath[ch][p // tbc]
                    prod = dot0(blk_ref[0, 0, k], rhs)
                    alive = k < live_ref[0, 0]
                    for j in range(tbc):
                        acc_ref[j * blk:(j + 1) * blk] += jnp.where(alive & (p % tbc == j), prod, 0.0)
                return carry

            lax.fori_loop(0, cap // group, turn, 0)
            cbuf[ch] = acc_ref[...].astype(BF).reshape(n_row, rows, fc)
        return [send(cbuf.at[ch, (me_r + d) % n_row], rbuf.at[ch, d - 1], c_s.at[ch, d - 1], c_r.at[ch, d - 1], row_id(d))
                for d in range(1, n_row)]

    total = None

    def project(ch, cps):
        for c in cps:
            c.wait_recv()
        s = cbuf[ch, me_r].astype(F32)
        for d in range(1, n_row):
            s += rbuf[ch, d - 1].astype(F32)
        return lax.dot_general(s.astype(BF), w_ref[:, ch * fc:(ch + 1) * fc], (((1,), (1,)), ((), ())),
                               preferred_element_type=F32)

    base = core * half
    at_row = pl.ds(pl.multiple_of(base + me_r * piece, piece), piece)
    at_me = pl.ds(pl.multiple_of(base + me_r * piece + (z * part if scatter else 0), part), part)

    def z_sum():
        for c in zz_cp:
            c.wait_recv()
        acc = zpick[0][...].astype(F32)
        for d in range(1, n_z):
            acc += zrecv[d - 1].astype(F32)
        gb_ref[...] = jnp.sum(acc[part:], axis=0, keepdims=True)
        gw[at_me] = acc[:part].astype(BF)
        if not scatter:
            return []
        return [send(gw.at[at_me], gw.at[at_me], wz_s.at[d - 1], wz_r.at[d - 1], z_id(d)) for d in range(1, n_z)]

    fw = forward(0)
    wz_cp = z_sum()
    c_cp = [contribute(0, fw)]
    for c in wz_cp:
        c.wait_recv()
    wr_cp = [send(gw.at[at_row], gw.at[at_row], wr_s.at[d - 1], wr_r.at[d - 1], row_id(d)) for d in range(1, n_row)]
    wf_cp = [send(gw.at[at_row], gw.at[at_row], wf_s.at[0], wf_r.at[0], sib_id)]
    for ch in range(1, nch):
        fw = forward(ch)
        c_cp.append(contribute(ch, fw))
        more = project(ch - 1, c_cp[ch - 1])
        total = more if total is None else total + more
    for d in range(1, n_row):
        wr_cp[d - 1].wait_recv()
        src = pl.ds(pl.multiple_of(base + ((me_r + n_row - d) % n_row) * piece, piece), piece)
        wf_cp.append(send(gw.at[src], gw.at[src], wf_s.at[d], wf_r.at[d], sib_id))
    more = project(nch - 1, c_cp[nch - 1])
    total = more if total is None else total + more
    gi_ref[...] = total.astype(BF)
    for c in wf_cp:
        c.wait_recv()
    gw_ref[...] = gw[...]
    for c in sent:
        c.wait_send()


def body(n_row, n_col, grad_out, relu_mask, aggregated, weight, adj_blocks, block_pos, block_live):
    rows, feat = grad_out.shape
    cap, blk = adj_blocks.shape[2], adj_blocks.shape[-1]
    group = max(d for d in range(1, 17) if cap % d == 0)
    nch = 2
    fc = feat // nch
    n_z = n_col // 2
    piece = feat // 2 // n_row
    scatter = piece % (n_z * TILE) == 0
    part = piece // n_z if scatter else piece
    tbc = n_row * rows // blk
    if cap == group:
        lhs = pltpu.VMEM((cap * blk, tbc * blk), BF)
    else:
        lhs = pltpu.VMEM((tbc * blk, fc), F32)
    dma = pltpu.SemaphoreType.DMA
    scratch = [pltpu.VMEM((n_col, rows, fc), BF) for _ in range(nch)] + [
        lhs,
        pltpu.VMEM((nch, n_row, rows, fc), BF),
        pltpu.VMEM((nch, n_row - 1, rows, fc), BF),
        pltpu.VMEM((rows, feat // 2), BF),
        pltpu.VMEM((n_row, piece + TILE, feat), BF),
        pltpu.VMEM((n_row - 1, piece + TILE, feat), BF),
        pltpu.VMEM((n_z if scatter else 1, part + TILE, feat), BF),
        pltpu.VMEM((n_z - 1, part + TILE, feat), BF),
        pltpu.VMEM((feat, feat), BF),
    ]
    sems = [dma((nch, n_z)), dma((nch, n_z)), dma((nch, n_z - 1)), dma((nch, n_z - 1)),
            dma((nch, n_row - 1)), dma((nch, n_row - 1)), dma(()), dma(()),
            dma((n_row - 1,)), dma((n_row - 1,)), dma((n_z - 1,)), dma((n_z - 1,)),
            dma((n_z - 1,)), dma((n_z - 1,)), dma((n_row - 1,)), dma((n_row - 1,)),
            dma((n_row,)), dma((n_row,))]
    vm = pl.BlockSpec(memory_space=pltpu.VMEM)
    sm = pl.BlockSpec(memory_space=pltpu.SMEM)
    gi, gw, gb = pl.pallas_call(
        functools.partial(kernel, (n_row, n_col, nch, cap, group, scatter)),
        out_shape=(jax.ShapeDtypeStruct((rows, feat), BF),
                   jax.ShapeDtypeStruct((feat, feat), BF),
                   jax.ShapeDtypeStruct((1, feat), F32)),
        in_specs=[vm, vm, vm, vm, vm, sm, sm],
        out_specs=(vm, vm, vm),
        scratch_shapes=scratch + sems,
        compiler_params=pltpu.CompilerParams(collective_id=0, has_side_effects=True,
                                             vmem_limit_bytes=48 * 1024 * 1024),
    )(grad_out, relu_mask, aggregated, weight, adj_blocks, block_pos, block_live)
    factor = 1.0 / math.sqrt(rows * n_row * n_col)
    return gi.reshape(1, rows, feat), gw.astype(F32) * factor, gb.reshape(feat) * factor


def solution(mesh):
    return jax.shard_map(
        functools.partial(body, mesh.shape["row"], mesh.shape["col"]),
        mesh=mesh,
        in_specs=(
            P(("row", "col"), None),
            P(("row", "col"), None),
            P(("row", "col"), None),
            P(),
            P("row", "col", None, None, None),
            P("row", "col", None),
            P("row", "col"),
        ),
        out_specs=(P("col", "row", None), P(), P()),
        check_vma=False,
    )
```

time: 163 us -> 41.7 us (0.26)
  waiting for transfers between devices: 89.3 us -> 0 us
  blocking collectives: 39.9 us -> 0 us
  Pallas kernels: 0 us -> 33.1 us
  between operations: 16.2 us -> 1.33 us
  matrix products: 5.7 us -> 0 us
  other arithmetic: 4.67 us -> 1.69 us
    psum x1 -> x0, waiting for transfers between devices: 65.9 us -> none  [body(): lax.psum((weight_terms, bias_terms), ('row', 'col'))]
    psum x1 -> x0, blocking collectives: 39.9 us -> none  [body(): lax.psum((weight_terms, bias_terms), ('row', 'col'))]
    pallas_call x0 -> x1, Pallas kernels: none -> 33.1 us  [body(): pl.pallas_call(functools.partial(kernel, (n_row, n_col, nch, cap, group,...]
    all_gather x1 -> x0, waiting for transfers between devices: 23.4 us -> none  [body(): row_block = lax.all_gather(projected, 'col', axis=0, tiled=True)]
    dot_general x4 -> x0, matrix products: 5.7 us -> none  [the longest x1 2.2 us: body(): jnp.einsum('nf,ng->fg', aggregated, grad_pre, preferred_element_type=jnp....]
    unnamed x7 -> x13, local copies, waits for them, and re-layouts: 1.32 us -> 5.37 us
    dot_general x2 -> x0, local copies, waits for them, and re-layouts: 3.43 us -> none  [the longest x1 2.13 us: add_group(): jnp.einsum('kab,kaf->kbf', part_blocks, selected_row_set, preferred_eleme...]
    gather x1 -> x0, local copies, waits for them, and re-layouts: 1.82 us -> none  [add_group(): selected_row_set = stacked_tiles[part_slots // tile_cols]]
  transfers between devices with their start and end apart: 3 -> 0, of which waited for: 2 -> 0; matrix products, arithmetic and copies ran while one was open for 8% -> 0% of each run, Pallas kernels for 0% -> 0%
where the time goes in v1:
time: 41.7 us; the launch traced here: 41.4 us
  Pallas kernels  33.1 us (79%)
  local copies, waits for them, and re-layouts  5.37 us (13%)
  other arithmetic  1.69 us (4%)
  between operations  1.33 us (3%)
    pallas_call x1, Pallas kernels, body(): pl.pallas_call(functools.partial(kernel, (n_row, n_col, nch, cap, group,...  33.1 us
    unnamed x13, local copies, waits for them, and re-layouts  5.37 us
    mul x1, other arithmetic, body(): gw.astype(F32) * factor  1.11 us

profile of v1, /device:TPU:0, one launch (start us, length us, event | category | flops | bytes accessed | tf_op | source)
XLA Modules:
  0.0 41.4 jit_solution(14618280209564602038)
XLA Ops:
  0.6 0.0 copy-start.5
  1.3 0.0 copy-done.5
  1.3 0.0 copy-start
  1.3 1.0 %copy-done = bf16[512,512]{1,0:T(8,128)(2,1)S(1)} copy-done((bf16[512,512]{1,0:T(8,128)(2,1)S(1)}, bf16[512,512]{1,0:T(8,128)(2,1)}, u32[]{:S(2)}) %copy-start) | copy-done | bytes 524312
  2.4 0.0 copy-start.1
  2.4 0.9 %copy-done.1 = s32[128,512]{1,0:T(8,128)S(1)} copy-done((s32[128,512]{1,0:T(8,128)S(1)}, s32[128,512]{1,0:T(8,128)}, u32[]{:S(2)}) %copy-start.1) | copy-done | bytes 262168
  3.3 0.0 copy-start.2
  3.3 0.9 %copy-done.2 = bf16[1,1,5,128,128]{4,3,2,1,0:T(8,128)(2,1)S(1)} copy-done((bf16[1,1,5,128,128]{4,3,2,1,0:T(8,128)(2,1)S(1)}, bf16[1,1,5,128,128]{4,3,2,1,0:T(8,128)(2,1)}, u32[]{:S(2)}) %copy-start.2) | copy-done | bytes 163864
  4.2 0.0 copy-start.3
  4.2 0.9 %copy-done.3 = bf16[128,512]{1,0:T(8,128)(2,1)S(1)} copy-done((bf16[128,512]{1,0:T(8,128)(2,1)S(1)}, bf16[128,512]{1,0:T(8,128)(2,1)}, u32[]{:S(2)}) %copy-start.3) | copy-done | bytes 131096
  5.1 0.0 copy-start.4
  5.1 0.9 %copy-done.4 = bf16[128,512]{1,0:T(8,128)(2,1)S(1)} copy-done((bf16[128,512]{1,0:T(8,128)(2,1)S(1)}, bf16[128,512]{1,0:T(8,128)(2,1)}, u32[]{:S(2)}) %copy-start.4) | copy-done | bytes 131096
  6.0 33.1 %shard_map.94 = (bf16[128,512]{1,0:T(8,128)(2,1)S(1)}, bf16[512,512]{1,0:T(8,128)(2,1)S(1)}, f32[1,512]{1,0:T(1,128)S(1)}) custom-call(bf16[128,512]{1,0:T(8,128)(2,1)S(1)} %copy-done.3, s32[128,512]{1,0:T(8,128)S(1)} %copy-done.1, bf16[128,512]{1,0:T(8,128)(2,1)S(1)} %copy-done.4, bf16[512,512]{1,0:T(8,128)(2,1)S(1)} %copy-done, ...), custom_call_target="tpu_custom_call" | custom-call | tf_op jit(solution)/shard_map/pallas_call | solution.py:243
  39.1 0.6 %broadcast_multiply_fusion = f32[1,512]{1,0:T(1,128)} fusion(f32[1,512]{1,0:T(1,128)S(1)} %get-tuple-element.8), kind=kLoop, calls=%fused_computation.1 | loop fusion | flops 512 | bytes 4096 | tf_op jit(solution)/shard_map/mul | solution.py:255
  39.7 1.1 %convert_multiply_fusion = f32[512,512]{1,0:T(8,128)} fusion(bf16[512,512]{1,0:T(8,128)(2,1)S(1)} %get-tuple-element.7), kind=kLoop, calls=%fused_computation | loop fusion | flops 524288 | bytes 1572864 | tf_op jit(solution)/shard_map/mul | solution.py:255
  40.8 0.7 %copy.12 = bf16[1,128,512]{2,1,0:T(8,128)(2,1)} copy(bf16[1,128,512]{2,1,0:T(8,128)(2,1)S(1)} %bitcast.2) | data formatting | bytes 262144
Async XLA Ops:
  0.6 0.7 %copy-start.5 = (s32[1,1,5]{2,1,0:T(1,128)S(1)}, s32[1,1,5]{2,1,0:T(1,128)}, u32[]{:S(2)}) copy-start(s32[1,1,5]{2,1,0:T(1,128)} %pos_ref.1) | copy-start | bytes 64
  1.3 1.0 %copy-start = (bf16[512,512]{1,0:T(8,128)(2,1)S(1)}, bf16[512,512]{1,0:T(8,128)(2,1)}, u32[]{:S(2)}) copy-start(bf16[512,512]{1,0:T(8,128)(2,1)} %w_ref.1) | copy-start | bytes 1572868
  2.4 0.9 %copy-start.1 = (s32[128,512]{1,0:T(8,128)S(1)}, s32[128,512]{1,0:T(8,128)}, u32[]{:S(2)}) copy-start(s32[128,512]{1,0:T(8,128)} %mask_ref.1) | copy-start | bytes 786436
  3.3 0.9 %copy-start.2 = (bf16[1,1,5,128,128]{4,3,2,1,0:T(8,128)(2,1)S(1)}, bf16[1,1,5,128,128]{4,3,2,1,0:T(8,128)(2,1)}, u32[]{:S(2)}) copy-start(bf16[1,1,5,128,128]{4,3,2,1,0:T(8,128)(2,1)} %blk_ref.1) | copy-start | bytes 491524
  4.2 0.9 %copy-start.3 = (bf16[128,512]{1,0:T(8,128)(2,1)S(1)}, bf16[128,512]{1,0:T(8,128)(2,1)}, u32[]{:S(2)}) copy-start(bf16[128,512]{1,0:T(8,128)(2,1)} %go_ref.1) | copy-start | bytes 393220
  5.1 0.9 %copy-start.4 = (bf16[128,512]{1,0:T(8,128)(2,1)S(1)}, bf16[128,512]{1,0:T(8,128)(2,1)}, u32[]{:S(2)}) copy-start(bf16[128,512]{1,0:T(8,128)(2,1)} %agg_ref.1) | copy-start | bytes 393220

commit v2 on v1

--- a/solution.py
+++ b/solution.py
@@ -23,8 +23,9 @@
     n_row, n_col, nch, cap, group, scatter = cfg
     n_z = n_col // 2
     gath = scr[:nch]
-    lhs, cbuf, rbuf, asib, gpart, grecv, zsend, zrecv, gw = scr[nch:nch + 9]
-    ag_s, ag_r, fw_s, fw_r, c_s, c_r, as_s, as_r, g_s, g_r, z_s, z_r, wz_s, wz_r, wr_s, wr_r, wf_s, wf_r = scr[nch + 9:]
+    lhs, cbuf, rbuf, asib, gpart, grecv, zsend, zrecv, gw, go_v, mask_v, agg_v, w_v, blk_v, bsend, brecv = scr[nch:nch + 16]
+    (ag_s, ag_r, fw_s, fw_r, c_s, c_r, as_s, as_r, g_s, g_r, z_s, z_r, wz_s, wz_r, wr_s, wr_r, wf_s, wf_r,
+     b_s, b_r, in_s) = scr[nch + 16:]
     rows, feat = go_ref.shape
     fc = feat // nch
     blk = blk_ref.shape[-1]
@@ -43,6 +44,13 @@
     def z_id(d):
         return (me_r, ((z + d) % n_z) * 2 + core)
 
+    other = pl.ds(pl.multiple_of((1 - core) * half, half), half)
+    mine = pl.ds(pl.multiple_of(core * half, half), half)
+    loads = [pltpu.make_async_copy(src, dst, in_s.at[i]) for i, (src, dst) in enumerate((
+        (go_ref, go_v), (mask_ref, mask_v), (agg_ref.at[:, mine], agg_v), (blk_ref.at[0, 0], blk_v), (w_ref, w_v)))]
+    for c in loads:
+        c.start()
+
     sent = []
 
     def send(src, dst, s, r, dev):
@@ -57,65 +65,46 @@
     for p in peers:
         pl.semaphore_signal(barrier, inc=1, device_id=p, device_id_type=MESH)
 
+    loads[0].wait()
+    loads[1].wait()
     for ch in range(nch):
         cols = slice(ch * fc, (ch + 1) * fc)
-        gath[ch][me_c] = go_ref[:, cols] * mask_ref[:, cols].astype(F32).astype(BF)
+        gath[ch][me_c] = go_v[:, cols] * mask_v[:, cols].astype(F32).astype(BF)
 
     pl.semaphore_wait(barrier, len(peers))
 
     sib_cp, z_cp = [], []
-    other = pl.ds(pl.multiple_of((1 - core) * half, half), half)
-    mine = pl.ds(pl.multiple_of(core * half, half), half)
     agg_cp = send(agg_ref.at[:, other], asib, as_s, as_r, sib_id)
     for ch in range(nch):
         own = gath[ch].at[me_c]
         sib_cp.append(send(own, own, ag_s.at[ch, 0], ag_r.at[ch, 0], sib_id))
         z_cp.append([send(own, own, ag_s.at[ch, d], ag_r.at[ch, d], z_id(d)) for d in range(1, n_z)])
 
+    loads[2].wait()
     agg_cp.wait_recv()
-    bias = jnp.zeros((1, feat), F32)
-    sums = []
     for ch in range(nch):
         cols = slice(ch * fc, (ch + 1) * fc)
         sib_cp[ch].wait_recv()
-        a, b = gath[ch][me_c], gath[ch][sib]
-        g = dot0(agg_ref[:, mine], a) + dot0(asib[...], b)
-        gpart[:, 0:piece, cols] = g.astype(BF).reshape(n_row, piece, fc)
-        sums.append(jnp.sum(a.astype(F32) + b.astype(F32), axis=0, keepdims=True))
-    bias = jnp.concatenate(sums, axis=1)
-
-    def two_rows(v):
-        hi = v.astype(BF).astype(F32)
-        ids = lax.broadcasted_iota(jnp.int32, (TILE, feat), 0)
-        return jnp.where(ids == 0, hi, jnp.where(ids == 1, v - hi, 0.0)).astype(BF)
-
-    tail = two_rows(bias)
-    for r in range(n_row):
-        gpart[r, piece:piece + TILE, :] = tail
+        g = dot0(agg_v[...], gath[ch][me_c]) + dot0(asib[...], gath[ch][sib])
+        gpart[:, :, cols] = g.astype(BF).reshape(n_row, piece, fc)
     g_cp = [send(gpart.at[(me_r + d) % n_row], grecv.at[d - 1], g_s.at[d - 1], g_r.at[d - 1], row_id(d))
             for d in range(1, n_row)]
 
+    loads[3].wait()
     if cap == group:
         for k in range(cap):
             at = pos_ref[0, 0, k] % tbc
             alive = k < live_ref[0, 0]
             for j in range(tbc):
                 lhs[k * blk:(k + 1) * blk, j * blk:(j + 1) * blk] = jnp.where(
-                    alive & (at == j), blk_ref[0, 0, k], jnp.zeros((blk, blk), BF))
+                    alive & (at == j), blk_v[k], jnp.zeros((blk, blk), BF))
 
     for c in g_cp:
         c.wait_recv()
     acc = gpart[me_r].astype(F32)
     for d in range(1, n_row):
         acc += grecv[d - 1].astype(F32)
-    tail = two_rows(jnp.sum(acc[piece:], axis=0, keepdims=True))
-    if scatter:
-        zsend[:, 0:part] = acc[:piece].astype(BF).reshape(n_z, part, feat)
-        for q in range(n_z):
-            zsend[q, part:] = tail
-    else:
-        zsend[0, 0:part] = acc[:piece].astype(BF)
-        zsend[0, part:] = tail
+    zsend[...] = acc.astype(BF).reshape(zsend.shape)
     zpick = [zsend.at[(z + d) % n_z if scatter else 0] for d in range(n_z)]
     zz_cp = [send(zpick[d], zrecv.at[d - 1], z_s.at[d - 1], z_r.at[d - 1], z_id(d)) for d in range(1, n_z)]
 
@@ -142,7 +131,7 @@
                     k = t * group + i
                     p = pos_ref[0, 0, k]
                     rhs = gath[ch][p // tbc]
-                    prod = dot0(blk_ref[0, 0, k], rhs)
+                    prod = dot0(blk_v[k], rhs)
                     alive = k < live_ref[0, 0]
                     for j in range(tbc):
                         acc_ref[j * blk:(j + 1) * blk] += jnp.where(alive & (p % tbc == j), prod, 0.0)
@@ -161,7 +150,7 @@
         s = cbuf[ch, me_r].astype(F32)
         for d in range(1, n_row):
             s += rbuf[ch, d - 1].astype(F32)
-        return lax.dot_general(s.astype(BF), w_ref[:, ch * fc:(ch + 1) * fc], (((1,), (1,)), ((), ())),
+        return lax.dot_general(s.astype(BF), w_v[:, ch * fc:(ch + 1) * fc], (((1,), (1,)), ((), ())),
                                preferred_element_type=F32)
 
     base = core * half
@@ -174,23 +163,34 @@
         acc = zpick[0][...].astype(F32)
         for d in range(1, n_z):
             acc += zrecv[d - 1].astype(F32)
-        gb_ref[...] = jnp.sum(acc[part:], axis=0, keepdims=True)
-        gw[at_me] = acc[:part].astype(BF)
+        gw[at_me] = acc.astype(BF)
         if not scatter:
             return []
         return [send(gw.at[at_me], gw.at[at_me], wz_s.at[d - 1], wz_r.at[d - 1], z_id(d)) for d in range(1, n_z)]
 
-    fw = forward(0)
+    lanes = 128
+    c_cp = [contribute(0, forward(0))]
     wz_cp = z_sum()
-    c_cp = [contribute(0, fw)]
+    for ch in range(1, nch):
+        c_cp.append(contribute(ch, forward(ch)))
     for c in wz_cp:
         c.wait_recv()
     wr_cp = [send(gw.at[at_row], gw.at[at_row], wr_s.at[d - 1], wr_r.at[d - 1], row_id(d)) for d in range(1, n_row)]
     wf_cp = [send(gw.at[at_row], gw.at[at_row], wf_s.at[0], wf_r.at[0], sib_id)]
-    for ch in range(1, nch):
-        fw = forward(ch)
-        c_cp.append(contribute(ch, fw))
-        more = project(ch - 1, c_cp[ch - 1])
+
+    bsend[...] = jnp.zeros_like(bsend)
+    ones = jnp.ones((TILE, n_col * rows), BF)
+    for ch in range(nch):
+        sums = lax.dot_general(ones, gath[ch][...].reshape(n_col * rows, fc), (((1,), (0,)), ((), ())),
+                               preferred_element_type=F32)
+        for i in range(fc // lanes):
+            at = ch * (fc // lanes) + i
+            bsend[at:at + 1, :] = sums[0:1, i * lanes:(i + 1) * lanes]
+    b_cp = [send(bsend, brecv.at[d - 1], b_s.at[d - 1], b_r.at[d - 1], row_id(d)) for d in range(1, n_row)]
+
+    loads[4].wait()
+    for ch in range(nch - 1):
+        more = project(ch, c_cp[ch])
         total = more if total is None else total + more
     for d in range(1, n_row):
         wr_cp[d - 1].wait_recv()
@@ -199,6 +199,11 @@
     more = project(nch - 1, c_cp[nch - 1])
     total = more if total is None else total + more
     gi_ref[...] = total.astype(BF)
+    bias = bsend[...]
+    for d in range(1, n_row):
+        b_cp[d - 1].wait_recv()
+        bias += brecv[d - 1]
+    gb_ref[...] = bias
     for c in wf_cp:
         c.wait_recv()
     gw_ref[...] = gw[...]
@@ -217,6 +222,7 @@
     scatter = piece % (n_z * TILE) == 0
     part = piece // n_z if scatter else piece
     tbc = n_row * rows // blk
+    brows = -(-feat // 1024) * 8
     if cap == group:
         lhs = pltpu.VMEM((cap * blk, tbc * blk), BF)
     else:
@@ -227,32 +233,40 @@
         pltpu.VMEM((nch, n_row, rows, fc), BF),
         pltpu.VMEM((nch, n_row - 1, rows, fc), BF),
         pltpu.VMEM((rows, feat // 2), BF),
-        pltpu.VMEM((n_row, piece + TILE, feat), BF),
-        pltpu.VMEM((n_row - 1, piece + TILE, feat), BF),
-        pltpu.VMEM((n_z if scatter else 1, part + TILE, feat), BF),
-        pltpu.VMEM((n_z - 1, part + TILE, feat), BF),
+        pltpu.VMEM((n_row, piece, feat), BF),
+        pltpu.VMEM((n_row - 1, piece, feat), BF),
+        pltpu.VMEM((n_z if scatter else 1, part, feat), BF),
+        pltpu.VMEM((n_z - 1, part, feat), BF),
         pltpu.VMEM((feat, feat), BF),
+        pltpu.VMEM((rows, feat), BF),
+        pltpu.VMEM((rows, feat), jnp.int32),
+        pltpu.VMEM((rows, feat // 2), BF),
+        pltpu.VMEM((feat, feat), BF),
+        pltpu.VMEM((cap, blk, blk), BF),
+        pltpu.VMEM((brows, 128), F32),
+        pltpu.VMEM((n_row - 1, brows, 128), F32),
     ]
     sems = [dma((nch, n_z)), dma((nch, n_z)), dma((nch, n_z - 1)), dma((nch, n_z - 1)),
             dma((nch, n_row - 1)), dma((nch, n_row - 1)), dma(()), dma(()),
             dma((n_row - 1,)), dma((n_row - 1,)), dma((n_z - 1,)), dma((n_z - 1,)),
             dma((n_z - 1,)), dma((n_z - 1,)), dma((n_row - 1,)), dma((n_row - 1,)),
-            dma((n_row,)), dma((n_row,))]
+            dma((n_row,)), dma((n_row,)), dma((n_row - 1,)), dma((n_row - 1,)), dma((5,))]
     vm = pl.BlockSpec(memory_space=pltpu.VMEM)
+    hbm = pl.BlockSpec(memory_space=pl.ANY)
     sm = pl.BlockSpec(memory_space=pltpu.SMEM)
     gi, gw, gb = pl.pallas_call(
         functools.partial(kernel, (n_row, n_col, nch, cap, group, scatter)),
         out_shape=(jax.ShapeDtypeStruct((rows, feat), BF),
                    jax.ShapeDtypeStruct((feat, feat), BF),
-                   jax.ShapeDtypeStruct((1, feat), F32)),
-        in_specs=[vm, vm, vm, vm, vm, sm, sm],
+                   jax.ShapeDtypeStruct((brows, 128), F32)),
+        in_specs=[hbm, hbm, hbm, hbm, hbm, sm, sm],
         out_specs=(vm, vm, vm),
         scratch_shapes=scratch + sems,
         compiler_params=pltpu.CompilerParams(collective_id=0, has_side_effects=True,
-                                             vmem_limit_bytes=48 * 1024 * 1024),
+                                             vmem_limit_bytes=56 * 1024 * 1024),
     )(grad_out, relu_mask, aggregated, weight, adj_blocks, block_pos, block_live)
     factor = 1.0 / math.sqrt(rows * n_row * n_col)
-    return gi.reshape(1, rows, feat), gw.astype(F32) * factor, gb.reshape(feat) * factor
+    return gi.reshape(1, rows, feat), gw.astype(F32) * factor, gb.reshape(-1)[:feat] * factor
 
 
 def solution(mesh):

time: 41.7 us -> 37.2 us (0.89)
  local copies, waits for them, and re-layouts: 5.37 us -> 1.34 us
  Pallas kernels: 33.1 us -> 31.5 us
  other arithmetic: 1.69 us -> 2.77 us
    unnamed x13 -> x5, local copies, waits for them, and re-layouts: 5.37 us -> 1.34 us
    pallas_call x1, Pallas kernels: 33.1 us -> 31.5 us  [body(): pl.pallas_call(functools.partial(kernel, (n_row, n_col, nch, cap, group,...]
    mul x1, other arithmetic: 1.11 us -> 2.19 us  [body(): gw.astype(F32) * factor]
where the time goes in v2:
time: 37.2 us; the launch traced here: 36.9 us
  Pallas kernels  31.5 us (85%)
  other arithmetic  2.77 us (7%)
  local copies, waits for them, and re-layouts  1.34 us (4%)
  between operations  1.3 us (3%)
    pallas_call x1, Pallas kernels, body(): pl.pallas_call(functools.partial(kernel, (n_row, n_col, nch, cap, group,...  31.5 us
    mul x1, other arithmetic, body(): gw.astype(F32) * factor  2.19 us
    unnamed x5, local copies, waits for them, and re-layouts  1.34 us

profile of v2, /device:TPU:0, one launch (start us, length us, event | category | flops | bytes accessed | tf_op | source)
XLA Modules:
  0.0 36.9 jit_solution(10986461966232270316)
XLA Ops:
  1.3 31.5 %shard_map.94 = (bf16[128,512]{1,0:T(8,128)(2,1)}, bf16[512,512]{1,0:T(8,128)(2,1)}, f32[8,128]{1,0:T(8,128)}) custom-call(bf16[128,512]{1,0:T(8,128)(2,1)} %go_ref.1, s32[128,512]{1,0:T(8,128)} %mask_ref.1, bf16[128,512]{1,0:T(8,128)(2,1)} %agg_ref.1, bf16[512,512]{1,0:T(8,128)(2,1)} %w_ref.1, bf16[1,1,5,128,128]{4,3,2,1,0:T(8,128)(2,1)} %blk_ref.1, ...), custom_call_target="tpu_custom_call" | custom-call | tf_op jit(solution)/shard_map/pallas_call | solution.py:257
  32.8 0.0 copy-start.1
  32.8 0.7 %copy-done.1 = f32[8,128]{1,0:T(8,128)S(1)} copy-done((f32[8,128]{1,0:T(8,128)S(1)}, f32[8,128]{1,0:T(8,128)}, u32[]{:S(2)}) %copy-start.1) | copy-done | bytes 4120
  33.5 0.6 %multiply_bitcast_fusion = f32[512]{0:T(512)} fusion(f32[8,128]{1,0:T(8,128)S(1)} %copy-done.1), kind=kLoop, calls=%fused_computation.1 | loop fusion | flops 512 | bytes 4096 | tf_op jit(solution)/shard_map/mul | solution.py:269
  34.1 0.0 copy-start
  34.1 2.2 %convert_multiply_fusion = f32[512,512]{1,0:T(8,128)} fusion(bf16[512,512]{1,0:T(8,128)(2,1)} %get-tuple-element.7), kind=kLoop, calls=%fused_computation | loop fusion | flops 524288 | bytes 1572864 | tf_op jit(solution)/shard_map/mul | solution.py:269
  36.3 0.0 copy-done
  36.3 0.7 %copy.12 = bf16[1,128,512]{2,1,0:T(8,128)(2,1)} copy(bf16[1,128,512]{2,1,0:T(8,128)(2,1)S(1)} %bitcast.3) | data formatting | bytes 262144
Async XLA Ops:
  32.8 0.7 %copy-start.1 = (f32[8,128]{1,0:T(8,128)S(1)}, f32[8,128]{1,0:T(8,128)}, u32[]{:S(2)}) copy-start(f32[8,128]{1,0:T(8,128)} %get-tuple-element.8) | copy-start | bytes 12292
  34.1 2.2 %copy-start = (bf16[128,512]{1,0:T(8,128)(2,1)S(1)}, bf16[128,512]{1,0:T(8,128)(2,1)}, u32[]{:S(2)}) copy-start(bf16[128,512]{1,0:T(8,128)(2,1)} %get-tuple-element.6) | copy-start | bytes 393220
